TPU v7x, 512 devices: a whole 4x8x8 slice. The times are simulated.
512 devices in a mesh: streams: 16 (over y, core), tp: 32 (over x, z).
Axes of the slice: x: 4, y: 8, z: 8, core: 2. Of those that a mesh axis runs over, the one named last changes fastest.
Arguments:
- hidden_in: bfloat16 [512, 4, 1024], P(('streams', 'tp')), may hold values from -6 to 6
- byte_qkv: bfloat16 [512, 4, 1536], P(('streams', 'tp'))
- byte_cache: bfloat16 [512, 256, 512], P(('streams', 'tp'))
- byte_len: int32 [512], P(('streams', 'tp')), may hold values from 2 to 256, as said below
- flags: int32 [512, 4], P(('streams', 'tp')), may hold values 0 or 1
- coarse_prev: bfloat16 [512, 1024], P(('streams', 'tp')), may hold values from -6 to 6
- owner_map: int32 [32, 16, 1], replicated, may hold values from 0 to 15; in each aligned block of 16 rows (0 to 15, 16 to 31, ..., all dimensions but the last counted through in order) at most 2 rows name the same one
- up_weight: bfloat16 [1024, 8192], P(None, 'tp'), may hold values from -0.1875 to 0.1875
- coarse_gain: float32 [8192], replicated, may hold values from 0.5 to 1.5
- query_weight: bfloat16 [8192, 4096], P(None, 'tp'), may hold values from -0.0625 to 0.0625
- keyval_weight: bfloat16 [8192, 1024], P('tp'), may hold values from -0.0625 to 0.0625
- return_weight: bfloat16 [4096, 1024], P('tp'), may hold values from -0.09375 to 0.09375
- coarse_cache: bfloat16 [16, 64, 32, 32, 256], P('streams', None, 'tp'), as said below
- coarse_len: int32 [16, 64], P('streams'), may hold values from 1 to 32, as said below
Outputs:
- byte_out: bfloat16 [512, 4, 1024], P(('streams', 'tp'))
Inputs may be any that keep to these rules, and one draw needn't show every extreme that they name: `owner_map`: within one index c of tp, no group owns more than 2 of the sequences s * 32 + c, and some group owns exactly 2. `byte_len`: some sequence has exactly 256 filled positions. `coarse_len`: some slot has exactly 32 filled positions. `coarse_cache`: the copies for heads h and h2 are equal where h // 8 = h2 // 8.
All inputs are finite; a program needn't handle non-finite values. No bound on the sum of `flags` on one device may be relied on, other than what follows from the above.
Results may differ from a plain program's by a relative error of at most 0.014.
Values may be sent and summed in bfloat16 or wider, within the bound.
A program may use at most 64 MiB of HBM per device.

v0:
```python
import jax
import jax.numpy as jnp
from jax import lax
from jax.sharding import PartitionSpec as P

HD = 128
OWNED_MOST = 2


EPSILON = 1e-05
NEG_FILL = -1e30


def split_softmax(scores_old, scores_new):
    largest = jnp.maximum(
        jnp.max(scores_old, axis=-1, keepdims=True), jnp.max(scores_new, axis=-1, keepdims=True)
    )
    exp_old = jnp.exp(scores_old - largest)
    exp_new = jnp.exp(scores_new - largest)
    denominator = jnp.sum(exp_old, axis=-1, keepdims=True) + jnp.sum(
        exp_new, axis=-1, keepdims=True
    )
    return (
        (exp_old / denominator).astype(jnp.bfloat16),
        (exp_new / denominator).astype(jnp.bfloat16),
    )


def rank_table(owner_map):
    owners = owner_map[:, :, 0]
    group_total = owners.shape[1]
    same_owner = owners[:, :, None] == owners[:, None, :]
    earlier = (
        jnp.arange(group_total, dtype=jnp.int32)[None, :, None]
        > jnp.arange(group_total, dtype=jnp.int32)[None, None, :]
    )
    ranking = jnp.sum((same_owner & earlier).astype(jnp.int32), axis=2)
    return (owners, ranking)


def byte_attention(byte_qkv, byte_cache, byte_len):
    number, step_count, total_width = byte_qkv.shape
    length = byte_cache.shape[1]
    kv_width = byte_cache.shape[2] // 2
    kv_groups = kv_width // HD
    head_count = (total_width - 2 * kv_width) // HD
    group_size = head_count // kv_groups
    query_part = byte_qkv[:, :, : head_count * HD].reshape(
        number, step_count, kv_groups, group_size, HD
    )
    new_keys = byte_qkv[:, :, head_count * HD : head_count * HD + kv_width].reshape(
        number, step_count, kv_groups, HD
    )
    new_values = byte_qkv[:, :, head_count * HD + kv_width :].reshape(
        number, step_count, kv_groups, HD
    )
    old_keys = byte_cache[:, :, :kv_width].reshape(number, length, kv_groups, HD)
    old_values = byte_cache[:, :, kv_width:].reshape(number, length, kv_groups, HD)
    scaling = HD ** (-0.5)
    scores_old = (
        jnp.einsum("nsgjd,nlgd->nsgjl", query_part, old_keys, preferred_element_type=jnp.float32)
        * scaling
    )
    valid_old = jnp.arange(length, dtype=jnp.int32)[None, :] < byte_len[:, None]
    scores_old = jnp.where(valid_old[:, None, None, None, :], scores_old, NEG_FILL)
    scores_new = (
        jnp.einsum("nsgjd,nugd->nsgju", query_part, new_keys, preferred_element_type=jnp.float32)
        * scaling
    )
    causal = jnp.arange(step_count)[:, None] >= jnp.arange(step_count)[None, :]
    scores_new = jnp.where(causal[None, :, None, None, :], scores_new, NEG_FILL)
    weights_old, weights_new = split_softmax(scores_old, scores_new)
    mixed_heads = jnp.einsum(
        "nsgjl,nlgd->nsgjd", weights_old, old_values, preferred_element_type=jnp.float32
    )
    mixed_heads = mixed_heads + jnp.einsum(
        "nsgju,nugd->nsgjd", weights_new, new_values, preferred_element_type=jnp.float32
    )
    return mixed_heads.reshape(number, step_count, head_count * HD)


def dispatch(block_rows, block_marks, owners, ranking):
    column_total = lax.axis_size("tp")
    row_index = lax.axis_index("streams")
    every_rows, every_marks = (
        lax.all_gather(block_rows, ("streams", "tp"), axis=0, tiled=True),
        lax.all_gather(block_marks, ("streams", "tp"), axis=0, tiled=True),
    )
    target = jnp.where(
        owners == row_index,
        jnp.arange(column_total, dtype=jnp.int32)[:, None] * OWNED_MOST + ranking,
        -1,
    )
    target_flat = target.T.reshape(-1)
    slot_ids = jnp.arange(column_total * OWNED_MOST, dtype=jnp.int32)
    picker = (slot_ids[:, None] == target_flat[None, :]).astype(jnp.bfloat16)
    slot_rows = jnp.einsum(
        "ai,ibd->abd", picker, every_rows, preferred_element_type=jnp.float32
    ).astype(jnp.bfloat16)
    slot_marks = jnp.einsum("ai,ib->ab", picker, every_marks, preferred_element_type=jnp.float32)
    return (slot_rows, slot_marks)


def coarse_project(slot_rows, up_weight, coarse_gain, query_weight, keyval_weight):
    column_total = lax.axis_size("tp")
    column = lax.axis_index("tp")
    part_width = up_weight.shape[1]
    expanded = jnp.einsum(
        "rbd,df->rbf", slot_rows, up_weight, preferred_element_type=jnp.float32
    ).astype(jnp.bfloat16)
    widened = lax.all_gather(expanded, "tp", axis=2, tiled=True).astype(jnp.float32)
    scaled_part = (widened * coarse_gain).astype(jnp.bfloat16)
    query_sum = jnp.einsum(
        "rbf,fh->rbh", scaled_part, query_weight, preferred_element_type=jnp.float32
    )
    squares = jnp.sum(widened * widened, axis=2)
    query_sum, squares = (query_sum, squares)
    own_gains = lax.dynamic_slice_in_dim(coarse_gain, column * part_width, part_width, 0)
    own_scaled = (expanded.astype(jnp.float32) * own_gains).astype(jnp.bfloat16)
    inverse = lax.rsqrt(squares / (part_width * column_total) + EPSILON)[:, :, None]
    queries = (query_sum * inverse).astype(jnp.bfloat16)
    kv_width = keyval_weight.shape[1]
    kv_heads = kv_width // (2 * HD)
    group_size = column_total // kv_heads
    head_group = column // group_size
    keyval_part = jnp.einsum(
        "rbf,fc->rbc", own_scaled, keyval_weight, preferred_element_type=jnp.float32
    )
    keyvals = lax.psum(keyval_part, "tp")
    new_keys = (lax.dynamic_slice_in_dim(keyvals, head_group * HD, HD, 2) * inverse).astype(
        jnp.bfloat16
    )
    new_values = (
        lax.dynamic_slice_in_dim(keyvals, (kv_heads + head_group) * HD, HD, 2) * inverse
    ).astype(jnp.bfloat16)
    return (queries, new_keys, new_values)


def coarse_attention(queries, step_ids, cache_own, cache_len, key_store, value_store, mark_store):
    length = cache_own.shape[1]
    step_count = key_store.shape[1]
    scaling = HD ** (-0.5)
    scores_old = (
        jnp.einsum(
            "rbd,rld->rbl", queries, cache_own[:, :, :HD], preferred_element_type=jnp.float32
        )
        * scaling
    )
    valid_old = jnp.arange(length, dtype=jnp.int32)[None, :] < cache_len[:, None]
    scores_old = jnp.where(valid_old[:, None, :], scores_old, NEG_FILL)
    scores_new = (
        jnp.einsum("rbd,rud->rbu", queries, key_store, preferred_element_type=jnp.float32) * scaling
    )
    valid_new = (jnp.arange(step_count)[None, None, :] <= step_ids[None, :, None]) & (
        mark_store[:, None, :] > 0.5
    )
    scores_new = jnp.where(valid_new, scores_new, NEG_FILL)
    weights_old, weights_new = split_softmax(scores_old, scores_new)
    mixed_heads = jnp.einsum(
        "rbl,rld->rbd", weights_old, cache_own[:, :, HD:], preferred_element_type=jnp.float32
    )
    mixed_heads = mixed_heads + jnp.einsum(
        "rbu,rud->rbd", weights_new, value_store, preferred_element_type=jnp.float32
    )
    return mixed_heads.astype(jnp.bfloat16)


def give_back(mixed_heads, return_weight, owners, ranking):
    row_index = lax.axis_index("streams")
    column = lax.axis_index("tp")
    summed = lax.psum_scatter(
        jnp.einsum("rbh,hd->rbd", mixed_heads, return_weight, preferred_element_type=jnp.float32),
        "tp",
        scatter_dimension=0,
        tiled=True,
    ).astype(jnp.bfloat16)
    every_back = lax.all_gather(summed, "streams", axis=0, tiled=True)
    my_owner = lax.dynamic_index_in_dim(
        lax.dynamic_index_in_dim(owners, column, 0, keepdims=False), row_index, 0, keepdims=False
    )
    my_rank = lax.dynamic_index_in_dim(
        lax.dynamic_index_in_dim(ranking, column, 0, keepdims=False), row_index, 0, keepdims=False
    )
    return lax.dynamic_index_in_dim(every_back, my_owner * OWNED_MOST + my_rank, 0, keepdims=False)


def shards(
    hidden_in,
    byte_qkv,
    byte_cache,
    byte_len,
    flags,
    coarse_prev,
    owner_map,
    up_weight,
    coarse_gain,
    query_weight,
    keyval_weight,
    return_weight,
    coarse_cache,
    coarse_len,
):
    step_count = hidden_in.shape[1]
    attended = byte_attention(byte_qkv, byte_cache, byte_len)
    byte_rows = (hidden_in.astype(jnp.float32) + attended).astype(jnp.bfloat16)
    byte_marks = flags.astype(jnp.bfloat16)
    owners, ranking = rank_table(owner_map)
    cache_own = coarse_cache[0, :, 0]
    cache_len = coarse_len[0]
    slot_rows, slot_marks = dispatch(byte_rows, byte_marks, owners, ranking)
    queries, new_keys, new_values = coarse_project(
        slot_rows, up_weight, coarse_gain, query_weight, keyval_weight
    )
    step_ids = jnp.arange(step_count, dtype=jnp.int32)
    mixed_heads = coarse_attention(
        queries, step_ids, cache_own, cache_len, new_keys, new_values, slot_marks
    )
    given_back = give_back(mixed_heads, return_weight, owners, ranking)
    current = coarse_prev[0].astype(jnp.float32)
    outputs = []
    for step in range(step_count):
        current = jnp.where(flags[0, step] > 0, given_back[step].astype(jnp.float32), current)
        outputs.append(byte_rows[0, step].astype(jnp.float32) + current)
    return jnp.stack(outputs)[None].astype(jnp.bfloat16)


def solution(mesh):
    return jax.shard_map(
        shards,
        mesh=mesh,
        in_specs=(
            P(("streams", "tp"), None, None),
            P(("streams", "tp"), None, None),
            P(("streams", "tp"), None, None),
            P(("streams", "tp")),
            P(("streams", "tp"), None),
            P(("streams", "tp"), None),
            P(),
            P(None, "tp"),
            P(),
            P(None, "tp"),
            P("tp", None),
            P("tp", None),
            P("streams", None, "tp", None, None),
            P("streams", None),
        ),
        out_specs=P(("streams", "tp"), None, None),
        check_vma=False,
    )
```

profile of v0, /device:TPU:1, one launch (start us, length us, event | category | flops | bytes accessed | tf_op | source)
XLA Modules:
  0.0 587.4 jit_solution(7376833832583837293)
XLA Ops:
  6.6 1.1 fusion.96
  7.9 0.7 slice.62
  9.3 0.9 convolution_multiply_fusion.2
  11.1 0.9 fusion.32
  12.0 0.7 fusion.61
  13.4 0.9 convert_reduce_fusion
  14.3 0.7 select_bitcast_fusion
  15.1 122.9 %all-gather.4.cloned.1.call-done = bf16[512,4,1024]{2,1,0:T(4,128)(2,1)} async-done(((bf16[1,4,1024]{2,1,0:T(4,128)(2,1)}), bf16[512,4,1024]{2,1,0:T(4,128)(2,1)}) %all-gather.4.cloned.1.call-update) | async-done | bytes 4194320 | tf_op jit(solution)/shard_map/all_gather | solution.py:86
  138.0 5.7 fusion.14
  143.8 1.2 fusion.100
  146.9 90.5 %all-gather = bf16[512,1,4]{2,1,0:T(2,128)(2,1)S(1)} all-gather(bf16[1,1,4]{2,1,0:T(2,128)(2,1)S(1)} %convert_bitcast_fusion), channel_id=1, replica_groups=mesh['streams'=16,'tp'=32] {'streams','tp'}, dimensions={0}, use_global_device_ids=true | all-gather | bytes 4104 | tf_op jit(solution)/shard_map/all_gather | solution.py:87
  237.6 0.7 fusion.97
  240.9 1.3 dynamic-slice.4
  243.1 2.2 fusion.35
  245.4 3.3 fusion.1
  248.8 1.2 fusion.23
  250.1 148.3 %all-reduce.4.cloned.1.call-done = f32[64,4,1024]{2,0,1:T(8,128)} async-done(((f32[64,4,1024]{2,0,1:T(8,128)}), f32[64,4,1024]{2,0,1:T(8,128)}) %all-reduce.4.cloned.1.call-update) | async-done | bytes 1048592 | tf_op jit(solution)/shard_map/psum | solution.py:129
  398.4 1.1 multiply_convert_fusion.2
  400.0 1.5 fusion.99
  402.5 1.4 fusion.28
  404.2 0.7 copy.161
  404.9 125.0 %all-reduce.5 = bf16[64,4,1024]{2,1,0:T(4,128)(2,1)} all-reduce(f32[64,4,1024]{2,1,0:T(4,128)S(1)} %copy.161), channel_id=2, replica_groups=mesh['streams'=16,'tp'=32] {'tp'}, use_global_device_ids=true, to_apply=%region_11.12.clone | all-reduce | flops 262144 | bytes 1572864
  529.9 0.7 dynamic-slice_convert_fusion
  530.6 49.6 %all_gather.15 = bf16[32,4,1024]{2,1,0:T(4,128)(2,1)S(1)} all-gather(bf16[2,4,1024]{2,1,0:T(4,128)(2,1)S(1)} %dynamic-slice_convert_fusion), channel_id=1, replica_groups=mesh['streams'=16,'tp'=32] {'streams'}, dimensions={0}, use_global_device_ids=true | all-gather | bytes 278528 | tf_op jit(solution)/shard_map/all_gather | solution.py:177
  (67 shorter events, 5.7 us)
Async XLA Ops:
  6.5 242.1 %copy-start = (bf16[8192,128]{1,0:T(8,128)(2,1)S(1)}, bf16[8192,128]{1,0:T(8,128)(2,1)}, u32[]{:S(2)}) copy-start(bf16[8192,128]{1,0:T(8,128)(2,1)} %param.23) | copy-start | bytes 6291460
  6.5 140.4 %copy-start.4 = (s32[1,4]{1,0:T(1,128)S(1)}, s32[1,4]{1,0:T(1,128)}, u32[]{:S(2)}) copy-start(s32[1,4]{1,0:T(1,128)} %param.18) | copy-start | bytes 52
  6.5 131.5 %all-gather.4.cloned.1.call-start = ((), (), s32[]{:S(2)}) async-start(), calls=%async_computation | async-start | bytes 4202496 | tf_op jit(solution)/shard_map/all_gather | solution.py:86
  6.5 234.3 %copy-start.7 = (f32[8192]{0:T(1024)S(1)}, f32[8192]{0:T(1024)}, u32[]{:S(2)}) copy-start(f32[8192]{0:T(1024)} %param.22) | copy-start | bytes 98308
  6.6 236.4 %copy-start.6 = (s32[1,64]{1,0:T(1,128)S(1)}, s32[1,64]{1,0:T(1,128)}, u32[]{:S(2)}) copy-start(s32[1,64]{1,0:T(1,128)} %param.27) | copy-start | bytes 772
  6.6 236.5 %copy-start.2 = (bf16[256,1024]{1,0:T(8,128)(2,1)S(1)}, bf16[256,1024]{1,0:T(8,128)(2,1)}, u32[]{:S(2)}) copy-start(bf16[256,1024]{1,0:T(8,128)(2,1)} %param.24) | copy-start | bytes 1572868
  13.3 232.0 %all-gather.6.cloned.1.call-start = ((), (), s32[]{:S(2)}) async-start(), calls=%async_computation.1 | async-start | bytes 4325376 | tf_op jit(solution)/shard_map/all_gather | solution.py:111
  143.7 254.7 %all-reduce.4.cloned.1.call-start = ((), (), s32[]{:S(2)}) async-start(), calls=%async_computation.2 | async-start | bytes 2097152 | tf_op jit(solution)/shard_map/psum | solution.py:129
  245.4 3.5 copy-start.1
  250.1 153.9 %copy-start.3 = (bf16[128,1024]{1,0:T(8,128)(2,1)S(1)}, bf16[128,1024]{1,0:T(8,128)(2,1)}, u32[]{:S(2)}) copy-start(bf16[128,1024]{1,0:T(8,128)(2,1)} %param.25) | copy-start | bytes 786436
  401.5 178.7 %copy-start.5 = (bf16[1,1024]{1,0:T(2,128)(2,1)S(1)}, bf16[1,1024]{1,0:T(2,128)(2,1)}, u32[]{:S(2)}) copy-start(bf16[1,1024]{1,0:T(2,128)(2,1)} %param.19) | copy-start | bytes 6148
Sparse Core Ops, SparseCore 0:
  13.5 124.5 all-gather.3
  143.8 85.0 all-gather.5
  245.4 152.8 all-reduce.3
where the time goes:
time: 588 us; the launch traced here: 587 us
  waiting for transfers between devices  271 us (46%)
  blocking collectives  265 us (45%)
  between operations  18.6 us (3%)
  matrix products  15 us (3%)
  other arithmetic  9.66 us (2%)
  local copies, waits for them, and re-layouts  7.67 us (1%)
    psum x1, waiting for transfers between devices, coarse_project(): keyvals = lax.psum(keyval_part, 'tp')  148 us
    unnamed x1, blocking collectives  125 us
    all_gather x1, waiting for transfers between devices, dispatch(): lax.all_gather(block_rows, ('streams', 'tp'), axis=0, tiled=True)  123 us
    all_gather x1, blocking collectives, dispatch(): lax.all_gather(block_marks, ('streams', 'tp'), axis=0, tiled=True)  90.5 us
    all_gather x1, blocking collectives, give_back(): every_back = lax.all_gather(summed, 'streams', axis=0, tiled=True)  49.6 us
  transfers between devices with their start and end apart: 3, of which 2 were waited for; matrix products, arithmetic and copies ran while one was open for 2% of the time, Pallas kernels for 0%

commit v1 on v0

v1 whole, which is shorter than its diff:
```python
import functools

import jax
import jax.numpy as jnp
from jax import lax
from jax.experimental import pallas as pl
from jax.experimental.pallas import tpu as pltpu
from jax.sharding import PartitionSpec as P

HD = 128
EPSILON = 1e-05
NEG_FILL = -1e30
F32, BF16, I32 = jnp.float32, jnp.bfloat16, jnp.int32
MESH = pl.DeviceIdType.MESH


def iota(shape, dim):
    return lax.broadcasted_iota(I32, shape, dim)


def dot(a, b):
    return lax.dot_general(a, b, (((1,), (0,)), ((), ())), preferred_element_type=F32)


def dot_t(a, b):
    return lax.dot_general(a, b, (((1,), (1,)), ((), ())), preferred_element_type=F32)


def bdot(a, b):
    return lax.dot_general(a, b, (((2,), (1,)), ((0,), (0,))), preferred_element_type=F32)


def bdot_t(a, b):
    return lax.dot_general(a, b, (((2,), (2,)), ((0,), (0,))), preferred_element_type=F32)


def kernel(
    S, X, Z,
    byte_len, flags, hidden, qkv, prev, owner_row, gain, coarse_len,
    byte_cache, up_hbm, query_hbm, keyval_hbm, return_hbm, cache_hbm,
    out_ref,
    bc, up, wq, wkv, wr, cc,
    qs, kn, os, xm,
    XS, XT, UT, MS, KP, KX, KZ, SQZ, SQX, PX, RX, PZ, RZ, RB,
    local_sem,
    xs_s, xs_r, ms_s, ms_r, rb_s, rb_r,
    xtz_s, xtz_r, xtx_s, xtx_r,
    utz_s, utz_r, utx_s, utx_r,
    kx_s, kx_r, kz_s, kz_r, sqz_s, sqz_r, sqx_s, sqx_r,
    px_s, px_r, pz_s, pz_r,
):
    T = X * Z
    me_s, me_t = lax.axis_index("streams"), lax.axis_index("tp")
    x, z = me_t // Z, me_t % Z
    rows_own = up.shape[0] // S

    locals_ = [
        pltpu.make_async_copy(up_hbm, up, local_sem.at[0]),
        pltpu.make_async_copy(byte_cache.at[0], bc, local_sem.at[1]),
        pltpu.make_async_copy(keyval_hbm, wkv, local_sem.at[2]),
        pltpu.make_async_copy(query_hbm, wq, local_sem.at[3]),
        pltpu.make_async_copy(cache_hbm.at[0, :, 0], cc, local_sem.at[4]),
        pltpu.make_async_copy(return_hbm, wr, local_sem.at[5]),
    ]
    for copy in locals_:
        copy.start()

    def s_peer(d):
        return (lax.rem(me_s + d, S), me_t)

    def z_peer(d):
        return (me_s, x * Z + lax.rem(z + d, Z))

    def x_peer(d):
        return (me_s, lax.rem(x + d, X) * Z + z)

    def loop(count, body):
        def step(d, carry):
            body(d)
            return carry

        lax.fori_loop(1, count, step, 0)

    def remote(src, dst, send, recv, peer):
        return pltpu.make_async_remote_copy(
            src_ref=src, dst_ref=dst, send_sem=send, recv_sem=recv,
            device_id=peer, device_id_type=MESH,
        )

    barrier = pltpu.get_barrier_semaphore()
    for count, peer in ((S, s_peer), (Z, z_peer), (X, x_peer)):
        loop(count, lambda d, peer=peer: pl.semaphore_signal(
            barrier, inc=1, device_id=peer(d), device_id_type=MESH))

    def spread(buf, me, count, peer, send, recv):
        loop(count, lambda d: remote(
            buf.at[me], buf.at[me], send.at[d], recv.at[d], peer(d)).start())

    def gathered(buf, me, count, peer, send, recv):
        def body(d):
            source = lax.rem(me + count - d, count)
            remote(buf.at[source], buf.at[source], send.at[d], recv.at[d], peer(d)).wait_recv()

        loop(count, body)

    def drained(buf, count, peer, send, recv):
        loop(count, lambda d: remote(
            buf.at[0], buf.at[0], send.at[d], recv.at[d], peer(d)).wait_send())

    def trade(src, dst, me, count, peer, send, recv):
        def body(d):
            other = lax.rem(me + d, count)
            remote(src.at[other], dst.at[me], send.at[d], recv.at[d], peer(d)).start()

        loop(count, body)

    def to_x(buf, zb, send, recv):
        loop(X, lambda d: remote(
            buf.at[x * Z + zb], buf.at[x * Z + zb],
            send.at[d, zb], recv.at[d, zb], x_peer(d)).start())

    def tp_start(buf, zs, zr, xs, xr):
        to_x(buf, z, xs, xr)
        loop(Z, lambda d: remote(
            buf.at[me_t], buf.at[me_t], zs.at[d], zr.at[d], z_peer(d)).start())

    def tp_forward(buf, zs, zr, xs, xr):
        def body(d):
            zb = lax.rem(z + Z - d, Z)
            block = buf.at[x * Z + zb]
            remote(block, block, zs.at[d], zr.at[d], z_peer(d)).wait_recv()
            to_x(buf, zb, xs, xr)

        loop(Z, body)

    def tp_arrived(buf, d, xs, xr):
        source = lax.rem(x + X - d, X)

        def body(zb, carry):
            block = buf.at[source * Z + zb]
            remote(block, block, xs.at[d, zb], xr.at[d, zb], x_peer(d)).wait_recv()
            return carry

        lax.fori_loop(0, Z, body, 0)

    def tp_drained(buf, zs, zr, xs, xr):
        drained(buf, Z, z_peer, zs, zr)

        def body(zb, carry):
            loop(X, lambda d: remote(
                buf.at[0], buf.at[0], xs.at[d, zb], xr.at[d, zb], x_peer(d)).wait_send())
            return carry

        lax.fori_loop(0, Z, body, 0)

    locals_[0].wait()
    own = up[pl.ds(pl.multiple_of(me_s * rows_own, rows_own), rows_own), :]
    UT[me_t] = (own.astype(F32) * gain[...]).astype(BF16)
    pl.semaphore_wait(barrier, S + Z + X - 3)
    tp_start(UT, utz_s, utz_r, utx_s, utx_r)

    locals_[2].wait()
    kv_heads = wkv.shape[1] // (2 * HD)
    partial = dot(UT[me_t], wkv[...]).astype(BF16)
    for j in range(kv_heads):
        KP[j] = jnp.concatenate(
            [partial[:, j * HD:(j + 1) * HD], partial[:, (kv_heads + j) * HD:(kv_heads + j + 1) * HD]],
            axis=1,
        )
    trade(KP, KX, x, X, x_peer, kx_s, kx_r)

    locals_[1].wait()
    steps = hidden.shape[1]
    kn[...] = jnp.zeros_like(kn)
    for i in range(2):
        for hh in range(4):
            qs[pl.ds(i * 16 + hh * 4, 4), :] = qkv[0, :, pl.ds((i * 4 + hh) * HD, HD)].astype(F32)
        kn[i, 0:4, :] = qkv[0, :, pl.ds((8 + i) * HD, HD)].astype(F32)
        kn[2 + i, 0:4, :] = qkv[0, :, pl.ds((10 + i) * HD, HD)].astype(F32)
    length = bc.shape[0]
    scaling = HD ** (-0.5)
    seen = iota((16, length), 1) < byte_len[0]
    causal = iota((16, 16), 1) <= iota((16, 16), 0) % 4
    for i in range(2):
        q_i = qs[pl.ds(i * 16, 16), :].astype(BF16)
        old = dot_t(q_i, bc[:, pl.ds(i * HD, HD)]) * scaling
        old = jnp.where(seen, old, NEG_FILL)
        new = dot_t(q_i, kn[i].astype(BF16)) * scaling
        new = jnp.where(causal, new, NEG_FILL)
        top = jnp.maximum(jnp.max(old, axis=1, keepdims=True), jnp.max(new, axis=1, keepdims=True))
        old, new = jnp.exp(old - top), jnp.exp(new - top)
        total = jnp.sum(old, axis=1, keepdims=True) + jnp.sum(new, axis=1, keepdims=True)
        old, new = (old / total).astype(BF16), (new / total).astype(BF16)
        os[pl.ds(i * 16, 16), :] = dot(old, bc[:, pl.ds((2 + i) * HD, HD)]) + dot(
            new, kn[2 + i].astype(BF16))
        for hh in range(4):
            xm[pl.ds((2 * i + hh // 2) * 4, 4), pl.ds((hh % 2) * HD, HD)] = (
                hidden[0, :, pl.ds((i * 4 + hh) * HD, HD)].astype(F32) + os[pl.ds(i * 16 + hh * 4, 4), :]
            )
    rows_16 = xm[...].astype(BF16)
    lanes = iota((16, HD), 1)
    marks = jnp.zeros((16, HD), F32)
    last = jnp.int32(-1)
    step_of_row = iota((16, 1), 0) % 4
    last_col = jnp.full((16, 1), -1, I32)
    for u in range(steps):
        mark = flags[0, u]
        marks = marks + jnp.where(lanes % 4 == u, mark.astype(F32), 0.0)
        last = jnp.where(mark > 0, jnp.int32(u), last)
        last_col = jnp.where(step_of_row == u, last, last_col)
    XS[me_s] = jnp.concatenate([rows_16, marks.astype(BF16)], axis=1)
    spread(XS, me_s, S, s_peer, xs_s, xs_r)

    tp_forward(UT, utz_s, utz_r, utx_s, utx_r)

    o_row = owner_row[...]
    eye = iota((S, S), 0) == iota((S, S), 1)
    o_col = jnp.sum(jnp.where(eye, o_row, 0.0), axis=1, keepdims=True)
    same = o_col == o_row
    rank_col = jnp.sum(
        jnp.where(same & (iota((S, S), 1) < iota((S, S), 0)), 1.0, 0.0), axis=1, keepdims=True)
    own_col = iota((S, 1), 0) == me_s
    my_owner = jnp.sum(jnp.where(own_col, o_col, 0.0), axis=0, keepdims=True)
    my_rank = jnp.sum(jnp.where(own_col, rank_col, 0.0), axis=0, keepdims=True)
    tgt_col = jnp.where(o_col == me_s.astype(F32), rank_col, -1.0)
    W = S * 16
    tgt = jnp.sum(
        jnp.where(iota((S, W), 1) // 16 == iota((S, W), 0), tgt_col, 0.0), axis=0, keepdims=True)

    gathered(XS, me_s, S, s_peer, xs_s, xs_r)
    r, l = iota((16, W), 0), iota((16, W), 1)
    every = XS[...].reshape(W, 256 + HD)
    picked = (tgt == ((r % 8) // 4).astype(F32)) & (l % 4 == r % 4)
    halves = []
    for part in range(2):
        pick = jnp.where(picked & ((l % 16) // 4 == (r // 8) * 2 + part), 1.0, 0.0).astype(BF16)
        halves.append(dot(pick, every[:, :256]).astype(BF16))
    slot_marks = []
    for j in range(2):
        pick = jnp.where((tgt == float(j)) & (l % 16 == 0), 1.0, 0.0).astype(BF16)
        slot_marks.append(dot(pick, every[:, 256:]))
    slot_marks = jnp.where((lanes % 8) // 4 == 0, slot_marks[0], slot_marks[1]).astype(BF16)
    XT[me_t] = jnp.concatenate(halves + [slot_marks], axis=1)
    tp_start(XT, xtz_s, xtz_r, xtx_s, xtx_r)

    def wait_trade(src, dst, me, count, peer, send, recv):
        def body(d):
            source = lax.rem(me + count - d, count)
            remote(src.at[0], dst.at[source], send.at[d], recv.at[d], peer(d)).wait_recv()

        loop(count, body)

    def total_of(own_part, buf, me, count):
        total = own_part.astype(F32)
        for d in range(1, count):
            total = total + buf[lax.rem(me + count - d, count)].astype(F32)
        return total

    wait_trade(KP, KX, x, X, x_peer, kx_s, kx_r)
    KZ[z] = total_of(KP[x], KX, x, X).astype(BF16)
    spread(KZ, z, Z, z_peer, kz_s, kz_r)

    tp_forward(XT, xtz_s, xtz_r, xtx_s, xtx_r)

    locals_[3].wait()

    def query_part(source, total):
        base = pl.multiple_of(source * (Z * 256), Z * 256)
        for zb in range(Z):
            total = total + dot(UT[source * Z + zb], wq[pl.ds(base + zb * 256, 256), :])
        return total

    folded = query_part(x, jnp.zeros((rows_own, HD), F32))
    for d in range(1, X):
        tp_arrived(UT, d, utx_s, utx_r)
        folded = query_part(lax.rem(x + X - d, X), folded)
    gathered(KZ, z, Z, z_peer, kz_s, kz_r)
    folded_kv = total_of(KZ[z], KZ, z, Z)
    MS[me_s] = jnp.concatenate([folded.astype(BF16), folded_kv.astype(BF16)], axis=1)
    spread(MS, me_s, S, s_peer, ms_s, ms_r)

    for d in range(1, X):
        tp_arrived(XT, d, xtx_s, xtx_r)
    rows_all = XT[:, :, :512].reshape(T * 16, 512)
    N = T * 8

    def project(top, bottom, width):
        upper = dot(rows_all, top).reshape(T, 16, width)[:, :8]
        lower = dot(rows_all, bottom).reshape(T, 16, width)[:, 8:]
        return (upper + lower).reshape(N, width)

    expanded = project(up[0:512, :], up[512:1024, :], up.shape[1]).astype(BF16).astype(F32)
    squared = expanded * expanded
    high = squared.astype(BF16)
    low = (squared - high.astype(F32)).astype(BF16)
    ones = jnp.ones((8, up.shape[1]), BF16)
    SQZ[z] = dot_t(ones, high) + dot_t(ones, low)
    spread(SQZ, z, Z, z_peer, sqz_s, sqz_r)
    gathered(SQZ, z, Z, z_peer, sqz_s, sqz_r)
    SQX[x] = total_of(SQZ[z], SQZ, z, Z)
    spread(SQX, x, X, x_peer, sqx_s, sqx_r)
    gathered(SQX, x, X, x_peer, sqx_s, sqx_r)
    squares = total_of(SQX[x], SQX, x, X)[0:1, :]
    inverse_row = lax.rsqrt(squares / (up.shape[1] * T) + EPSILON)
    inverse = jnp.sum(
        jnp.where(iota((N, N), 0) == iota((N, N), 1), inverse_row, 0.0), axis=1, keepdims=True)

    gathered(MS, me_s, S, s_peer, ms_s, ms_r)
    weights = MS[...].reshape(S * rows_own, 3 * HD)
    mixed = (project(weights[:512], weights[512:], 3 * HD) * inverse).astype(BF16)
    chunks = N // 32
    queries = mixed[:, :HD].reshape(chunks, 32, HD)
    keys = mixed[:, HD:2 * HD].reshape(chunks, 32, HD)
    values = mixed[:, 2 * HD:].reshape(chunks, 32, HD)

    locals_[4].wait()
    slots, span = cc.shape[0], cc.shape[1]
    cached = cc[...].reshape(chunks, 8 * span, 2 * HD)
    len_col = jnp.sum(
        jnp.where(iota((N, slots), 0) // 4 == iota((N, slots), 1), coarse_len[...].astype(F32), 0.0),
        axis=1, keepdims=True).reshape(chunks, 32, 1)
    wide = (32, 8 * span)
    position = jnp.where(
        iota(wide, 1) // span == iota(wide, 0) // 4, iota(wide, 1) % span, span).astype(F32)
    old = bdot_t(queries, cached[:, :, :HD]) * scaling
    old = jnp.where(position[None] < len_col, old, NEG_FILL)
    new = bdot_t(queries, keys) * scaling
    new_lane, new_row = iota((32, 32), 1), iota((32, 32), 0)
    allowed = (new_lane // 4 == new_row // 4) & (new_lane % 4 <= new_row % 4)
    mark_rows = []
    first_row = XT[:, 0:8, 512:].astype(F32).reshape(chunks, 4, 8, HD)
    for c in range(4):
        mark_rows.append(jnp.where(iota((1, 1, HD), 2) // 8 == c, first_row[:, c, 0:1, :], 0.0))
    mark_rows = (mark_rows[0] + mark_rows[1] + mark_rows[2] + mark_rows[3])[:, :, :32]
    new = jnp.where(allowed[None] & (mark_rows > 0.5), new, NEG_FILL)
    top = jnp.maximum(jnp.max(old, axis=2, keepdims=True), jnp.max(new, axis=2, keepdims=True))
    old, new = jnp.exp(old - top), jnp.exp(new - top)
    total = jnp.sum(old, axis=2, keepdims=True) + jnp.sum(new, axis=2, keepdims=True)
    old, new = (old / total).astype(BF16), (new / total).astype(BF16)
    attended = bdot(old, cached[:, :, HD:]) + bdot(new, values)
    attended = attended.astype(BF16).reshape(N, HD)

    locals_[5].wait()
    width = wr.shape[1]
    PX[...] = dot(attended, wr[...]).astype(BF16).reshape(X, Z * 8, width)
    trade(PX, RX, x, X, x_peer, px_s, px_r)
    wait_trade(PX, RX, x, X, x_peer, px_s, px_r)
    summed = total_of(PX[x], RX, x, X).reshape(Z, 8, width)
    PZ[...] = jnp.concatenate([summed[:, :, :512], summed[:, :, 512:]], axis=1).astype(BF16)
    trade(PZ, RZ, z, Z, z_peer, pz_s, pz_r)
    wait_trade(PZ, RZ, z, Z, z_peer, pz_s, pz_r)
    RB[me_s] = total_of(PZ[z], RZ, z, Z).astype(BF16)
    spread(RB, me_s, S, s_peer, rb_s, rb_r)
    gathered(RB, me_s, S, s_peer, rb_s, rb_r)

    back = RB[...].reshape(W, 512)
    lf = l.astype(F32)
    home = ((l // 16).astype(F32) == my_owner) & (((l % 8) // 4).astype(F32) == my_rank)
    home = home & (l % 4 == last_col) & ((l % 16) // 8 == r // 8)
    latest = jnp.zeros((16, 256), F32)
    for part in range(2):
        pick = jnp.where(home & ((r // 4) % 2 == part), 1.0, 0.0).astype(BF16)
        latest = latest + dot(pick, back[:, part * 256:(part + 1) * 256])
    earlier = jnp.zeros((16, 256), F32)
    for k in range(4):
        earlier = jnp.where(
            iota((16, 256), 0) // 4 == k, prev[0:1, pl.ds(k * 256, 256)].astype(F32), earlier)
    latest = jnp.where(last_col < 0, earlier, latest)
    xm[...] = rows_16.astype(F32) + latest
    for k in range(4):
        out_ref[0, :, pl.ds(k * 256, 256)] = xm[pl.ds(k * 4, 4), :].astype(BF16)

    for buf, count, peer, send, recv in (
        (XS, S, s_peer, xs_s, xs_r), (MS, S, s_peer, ms_s, ms_r), (RB, S, s_peer, rb_s, rb_r),
        (KX, X, x_peer, kx_s, kx_r), (KZ, Z, z_peer, kz_s, kz_r),
        (SQZ, Z, z_peer, sqz_s, sqz_r), (SQX, X, x_peer, sqx_s, sqx_r),
        (RX, X, x_peer, px_s, px_r), (RZ, Z, z_peer, pz_s, pz_r),
    ):
        drained(buf, count, peer, send, recv)
    tp_drained(UT, utz_s, utz_r, utx_s, utx_r)
    tp_drained(XT, xtz_s, xtz_r, xtx_s, xtx_r)


def shards(
    S, X, Z,
    hidden_in, byte_qkv, byte_cache, byte_len, flags, coarse_prev, owner_map, up_weight,
    coarse_gain, query_weight, keyval_weight, return_weight, coarse_cache, coarse_len,
):
    T = X * Z
    me_t = lax.axis_index("tp")
    part = up_weight.shape[1]
    gain = lax.dynamic_slice_in_dim(coarse_gain, me_t * part, part, 0)[None]
    owner_row = lax.dynamic_slice_in_dim(owner_map[:, :, 0], me_t, 1, 0).astype(F32)
    rows = up_weight.shape[0] // S
    heads2 = 2 * HD
    vm = pl.BlockSpec(memory_space=pltpu.VMEM)
    sm = pl.BlockSpec(memory_space=pltpu.SMEM)
    hbm = pl.BlockSpec(memory_space=pl.ANY)
    dma = pltpu.SemaphoreType.DMA
    pair = lambda *shape: [dma(shape), dma(shape)]
    scratch = [
        pltpu.VMEM(byte_cache.shape[1:], BF16),
        pltpu.VMEM(up_weight.shape, BF16),
        pltpu.VMEM(query_weight.shape, BF16),
        pltpu.VMEM(keyval_weight.shape, BF16),
        pltpu.VMEM(return_weight.shape, BF16),
        pltpu.VMEM((coarse_cache.shape[1],) + coarse_cache.shape[3:], BF16),
        pltpu.VMEM((32, HD), F32),
        pltpu.VMEM((4, 16, HD), F32),
        pltpu.VMEM((32, HD), F32),
        pltpu.VMEM((16, 256), F32),
        pltpu.VMEM((S, 16, 256 + HD), BF16),
        pltpu.VMEM((T, 16, 512 + HD), BF16),
        pltpu.VMEM((T, rows, part), BF16),
        pltpu.VMEM((S, rows, 3 * HD), BF16),
        pltpu.VMEM((X, rows, heads2), BF16),
        pltpu.VMEM((X, rows, heads2), BF16),
        pltpu.VMEM((Z, rows, heads2), BF16),
        pltpu.VMEM((Z, 8, T * 8), F32),
        pltpu.VMEM((X, 8, T * 8), F32),
        pltpu.VMEM((X, Z * 8, 1024), BF16),
        pltpu.VMEM((X, Z * 8, 1024), BF16),
        pltpu.VMEM((Z, 16, 512), BF16),
        pltpu.VMEM((Z, 16, 512), BF16),
        pltpu.VMEM((S, 16, 512), BF16),
        dma((6,)),
    ]
    for shape in (
        (S,), (S,), (S,), (Z,), (X, Z), (Z,), (X, Z), (X,), (Z,), (Z,), (X,), (X,), (Z,),
    ):
        scratch += pair(*shape)
    return pl.pallas_call(
        functools.partial(kernel, S, X, Z),
        out_shape=jax.ShapeDtypeStruct(hidden_in.shape, BF16),
        in_specs=[sm, sm] + [vm] * 6 + [hbm] * 6,
        out_specs=vm,
        scratch_shapes=scratch,
        compiler_params=pltpu.CompilerParams(
            collective_id=0, has_side_effects=True, vmem_limit_bytes=40 * 1024 * 1024
        ),
        name="decode",
    )(
        byte_len, flags, hidden_in, byte_qkv, coarse_prev, owner_row, gain, coarse_len,
        byte_cache, up_weight, query_weight, keyval_weight, return_weight, coarse_cache,
    )


def solution(mesh):
    S, T = mesh.shape["streams"], mesh.shape["tp"]
    X = 4 if T >= 16 else 2
    return jax.shard_map(
        functools.partial(shards, S, X, T // X),
        mesh=mesh,
        in_specs=(
            P(("streams", "tp"), None, None),
            P(("streams", "tp"), None, None),
            P(("streams", "tp"), None, None),
            P(("streams", "tp")),
            P(("streams", "tp"), None),
            P(("streams", "tp"), None),
            P(),
            P(None, "tp"),
            P(),
            P(None, "tp"),
            P("tp", None),
            P("tp", None),
            P("streams", None, "tp", None, None),
            P("streams", None),
        ),
        out_specs=P(("streams", "tp"), None, None),
        check_vma=False,
    )
```

time: 588 us -> 98.1 us (0.17)
  waiting for transfers between devices: 271 us -> 0 us
  blocking collectives: 265 us -> 0 us
  Pallas kernels: 0 us -> 84.3 us
  between operations: 18.6 us -> 0.67 us
  matrix products: 15 us -> 0 us
  other arithmetic: 9.66 us -> 0.98 us
    psum x1 -> x0, waiting for transfers between devices: 148 us -> none  [coarse_project(): keyvals = lax.psum(keyval_part, 'tp')]
    all_gather x2 -> x0, blocking collectives: 140 us -> none  [the longest x1 90.5 us: dispatch(): lax.all_gather(block_marks, ('streams', 'tp'), axis=0, tiled=True)]
    unnamed x1 -> x0, blocking collectives: 125 us -> none
    all_gather x2 -> x0, waiting for transfers between devices: 123 us -> none  [the longest x1 123 us: dispatch(): lax.all_gather(block_rows, ('streams', 'tp'), axis=0, tiled=True)]
    pallas_call x0 -> x1, Pallas kernels: none -> 84.3 us  [shards(): pl.pallas_call(functools.partial(kernel, S, X, Z), out_shape=jax.ShapeDty...]
    dot_general x13 -> x0, matrix products: 15 us -> none  [the longest x1 5.66 us: coarse_project(): jnp.einsum('rbd,df->rbf', slot_rows, up_weight, preferred_element_type=jn...]
    unnamed x19 -> x23, local copies, waits for them, and re-layouts: 1.67 us -> 10.8 us
  transfers between devices with their start and end apart: 3 -> 0, of which waited for: 2 -> 0; matrix products, arithmetic and copies ran while one was open for 2% -> 0% of each run, Pallas kernels for 0% -> 0%
where the time goes in v1:
time: 98.1 us; the launch traced here: 97.5 us
  Pallas kernels  84.3 us (86%)
  local copies, waits for them, and re-layouts  11.6 us (12%)
    pallas_call x1, Pallas kernels, shards(): pl.pallas_call(functools.partial(kernel, S, X, Z), out_shape=jax.ShapeDty...  84.3 us
    unnamed x23, local copies, waits for them, and re-layouts  10.8 us

profile of v1, /device:TPU:1, one launch (start us, length us, event | category | flops | bytes accessed | tf_op | source)
XLA Modules:
  0.0 97.5 jit_solution(16429026371238298355)
XLA Ops:
  0.7 1.0 %convert_reduce_fusion = f32[16]{0:T(128)S(1)} fusion(s32[32,16,1]{0,2,1:T(1,128)} %param.20, s32[]{:T(128)S(6)} %select_n.6), kind=kLoop, calls=%fused_computation | loop fusion | flops 16 | bytes 132 | tf_op jit(solution)/shard_map/convert_element_type | solution.py:393
  1.6 0.8 dynamic_slice.7
  2.4 0.0 copy-start
  2.4 1.6 %copy-done = bf16[8192,128]{1,0:T(8,128)(2,1)S(1)} copy-done((bf16[8192,128]{1,0:T(8,128)(2,1)S(1)}, bf16[8192,128]{1,0:T(8,128)(2,1)}, u32[]{:S(2)}) %copy-start) | copy-done | bytes 2097176
  4.0 0.0 copy-start.1
  4.0 1.2 %copy-done.1 = bf16[1,64,1,32,256]{4,3,2,1,0:T(8,128)(2,1)S(1)} copy-done((bf16[1,64,1,32,256]{4,3,2,1,0:T(8,128)(2,1)S(1)}, bf16[1,64,1,32,256]{4,3,2,1,0:T(8,128)(2,1)}, u32[]{:S(2)}) %copy-start.1) | copy-done | bytes 1048600
  5.2 0.0 copy-start.2
  5.2 1.0 %copy-done.2 = bf16[1024,256]{1,0:T(8,128)(2,1)S(1)} copy-done((bf16[1024,256]{1,0:T(8,128)(2,1)S(1)}, bf16[1024,256]{1,0:T(8,128)(2,1)}, u32[]{:S(2)}) %copy-start.2) | copy-done | bytes 524312
  6.3 0.0 copy-start.3
  6.3 1.0 %copy-done.3 = bf16[256,1024]{1,0:T(8,128)(2,1)S(1)} copy-done((bf16[256,1024]{1,0:T(8,128)(2,1)S(1)}, bf16[256,1024]{1,0:T(8,128)(2,1)}, u32[]{:S(2)}) %copy-start.3) | copy-done | bytes 524312
  7.3 0.0 copy-start.4
  7.3 0.9 copy-done.4
  8.3 0.0 copy-start.5
  8.3 0.9 copy-done.5
  9.2 0.0 copy-start.6
  9.2 0.7 copy-done.6
  9.9 0.0 copy-start.7
  9.9 0.7 copy-done.7
  10.6 0.0 copy-start.8
  10.6 0.7 copy-done.8
  11.3 0.7 copy-done.9
  12.0 0.7 copy-done.10
  12.6 84.3 %decode.1 = bf16[1,4,1024]{2,1,0:T(4,128)(2,1)S(1)} custom-call(s32[1]{0:T(128)S(6)} %copy.16.byte_len, s32[1,4]{1,0:T(1,128)S(1)} %copy-done.9, bf16[1,4,1024]{2,1,0:T(4,128)(2,1)S(1)} %copy-done.7, bf16[1,4,1536]{2,1,0:T(4,128)(2,1)S(1)} %copy-done.6, bf16[1,1024]{1,0:T(2,128)(2,1)S(1)} %copy-done.8, f32[1,16]{1,0:T(1,128)S(1)} %bitcast.3, ...), custom_call_target="tpu_custom_call" | custom-call | tf_op jit(solution)/shard_map/decode/pallas_call | solution.py:432
  96.9 0.6 copy.17
  (2 shorter events, 0.0 us)
Async XLA Ops:
  2.4 1.6 %copy-start = (bf16[8192,128]{1,0:T(8,128)(2,1)S(1)}, bf16[8192,128]{1,0:T(8,128)(2,1)}, u32[]{:S(2)}) copy-start(bf16[8192,128]{1,0:T(8,128)(2,1)} %query_hbm.1) | copy-start | bytes 6291460
  4.0 1.2 %copy-start.1 = (bf16[1,64,1,32,256]{4,3,2,1,0:T(8,128)(2,1)S(1)}, bf16[1,64,1,32,256]{4,3,2,1,0:T(8,128)(2,1)}, u32[]{:S(2)}) copy-start(bf16[1,64,1,32,256]{4,3,2,1,0:T(8,128)(2,1)} %cache_hbm.1) | copy-start | bytes 3145732
  5.2 1.0 %copy-start.2 = (bf16[1024,256]{1,0:T(8,128)(2,1)S(1)}, bf16[1024,256]{1,0:T(8,128)(2,1)}, u32[]{:S(2)}) copy-start(bf16[1024,256]{1,0:T(8,128)(2,1)} %up_hbm.1) | copy-start | bytes 1572868
  6.3 1.0 %copy-start.3 = (bf16[256,1024]{1,0:T(8,128)(2,1)S(1)}, bf16[256,1024]{1,0:T(8,128)(2,1)}, u32[]{:S(2)}) copy-start(bf16[256,1024]{1,0:T(8,128)(2,1)} %keyval_hbm.1) | copy-start | bytes 1572868
  7.3 0.9 copy-start.4
  8.3 0.9 copy-start.5
  9.2 0.7 copy-start.6
  9.9 0.7 copy-start.7
  10.6 0.7 copy-start.8
  11.3 0.7 copy-start.9
  12.0 0.7 copy-start.10

commit v2 on v1

v2 whole, which is shorter than its diff:
```python
import functools

import jax
import jax.numpy as jnp
from jax import lax
from jax.experimental import pallas as pl
from jax.experimental.pallas import tpu as pltpu
from jax.sharding import PartitionSpec as P

HD = 128
EPSILON = 1e-05
NEG_FILL = -1e30
F32, BF16, I32 = jnp.float32, jnp.bfloat16, jnp.int32
MESH = pl.DeviceIdType.MESH


def iota(shape, dim):
    return lax.broadcasted_iota(I32, shape, dim)


def dot(a, b):
    return lax.dot_general(a, b, (((1,), (0,)), ((), ())), preferred_element_type=F32)


def dot_t(a, b):
    return lax.dot_general(a, b, (((1,), (1,)), ((), ())), preferred_element_type=F32)


def bdot(a, b):
    return lax.dot_general(a, b, (((2,), (1,)), ((0,), (0,))), preferred_element_type=F32)


def bdot_t(a, b):
    return lax.dot_general(a, b, (((2,), (2,)), ((0,), (0,))), preferred_element_type=F32)


def kernel(
    S, X, Z,
    byte_len_hbm, flags_hbm, hidden_hbm, qkv_hbm, prev_hbm, owner_hbm, gain_hbm, len_hbm,
    byte_cache, up_hbm, query_hbm, keyval_hbm, return_hbm, cache_hbm,
    out_ref,
    byte_len, flags, hidden, qkv, prev, owners, gain, coarse_len,
    first, bc, up, wq, wkv, wr, ck, cv,
    qs, kn, os, xm, raw, cols,
    XS, XT, UT, MQ, MK, KP, KX, KS, KZ, KA, SQZ, SQX, PX, RX, PZ, RZ, RB,
    local_sem,
    xs_sems, xt_sems, ut_sems, mq_sems, mk_sems, rb_sems,
    kx_s, kx_r, kz_s, kz_r, ka_s, ka_r, sqz_s, sqz_r, sqx_s, sqx_r,
    px_s, px_r, pz_s, pz_r,
):
    T = X * Z
    me_s, me_t = lax.axis_index("streams"), lax.axis_index("tp")
    x, z = me_t // Z, me_t % Z
    Y = S // 2
    y, core = me_s // 2, me_s % 2
    me_p = core * Y + y
    rows_own = first.shape[0]

    small = [
        pltpu.make_async_copy(gain_hbm.at[me_t], gain, local_sem.at[6]),
        pltpu.make_async_copy(hidden_hbm, hidden, local_sem.at[7]),
        pltpu.make_async_copy(qkv_hbm, qkv, local_sem.at[8]),
        pltpu.make_async_copy(prev_hbm, prev, local_sem.at[9]),
        pltpu.make_async_copy(owner_hbm.at[:, 0, :], owners, local_sem.at[10]),
        pltpu.make_async_copy(len_hbm, coarse_len, local_sem.at[11]),
        pltpu.make_async_copy(byte_len_hbm, byte_len, local_sem.at[12]),
        pltpu.make_async_copy(flags_hbm, flags, local_sem.at[13]),
    ]
    locals_ = [
        pltpu.make_async_copy(up_hbm, up, local_sem.at[0]),
        pltpu.make_async_copy(byte_cache.at[0], bc, local_sem.at[1]),
        pltpu.make_async_copy(keyval_hbm, wkv, local_sem.at[2]),
        pltpu.make_async_copy(query_hbm, wq, local_sem.at[3]),
        pltpu.make_async_copy(cache_hbm.at[0, :, 0, :, pl.ds(0, HD)], ck, local_sem.at[4]),
        pltpu.make_async_copy(return_hbm, wr, local_sem.at[5]),
        pltpu.make_async_copy(cache_hbm.at[0, :, 0, :, pl.ds(HD, HD)], cv, local_sem.at[14]),
    ]
    own_up = pltpu.make_async_copy(
        up_hbm.at[pl.ds(pl.multiple_of(me_p * rows_own, rows_own), rows_own)], first, local_sem.at[15])
    own_up.start()
    for copy in small + [locals_[2], locals_[1]]:
        copy.start()

    def y_peer(d):
        return (lax.rem(y + d, Y) * 2 + core, me_t)

    def core_peer(d):
        return (y * 2 + lax.rem(core + d, 2), me_t)

    def z_peer(d):
        return (me_s, x * Z + lax.rem(z + d, Z))

    def x_peer(d):
        return (me_s, lax.rem(x + d, X) * Z + z)

    def loop(count, body):
        def step(d, carry):
            body(d)
            return carry

        lax.fori_loop(1, count, step, 0)

    def remote(src, dst, send, recv, peer):
        return pltpu.make_async_remote_copy(
            src_ref=src, dst_ref=dst, send_sem=send, recv_sem=recv,
            device_id=peer, device_id_type=MESH,
        )

    barrier = pltpu.get_barrier_semaphore()
    for count, peer in ((Y, y_peer), (2, core_peer), (Z, z_peer), (X, x_peer)):
        loop(count, lambda d, peer=peer: pl.semaphore_signal(
            barrier, inc=1, device_id=peer(d), device_id_type=MESH))

    comms = []

    class Axis:
        def __init__(self, src, dst, me, count, peer, send, recv):
            self.src, self.dst, self.me, self.count = src, dst, me, count
            self.peer, self.send, self.recv_sem = peer, send, recv
            self.received = False
            comms.append(self)

        def copy(self, d, src, dst):
            return remote(src, dst, self.send.at[d], self.recv_sem.at[d], self.peer(d))

        def start(self):
            def body(d):
                other = self.me if self.src is self.dst else lax.rem(self.me + d, self.count)
                self.copy(d, self.src.at[other], self.dst.at[self.me]).start()

            loop(self.count, body)
            return self

        def recv(self):
            def body(d):
                block = self.dst.at[lax.rem(self.me + self.count - d, self.count)]
                self.copy(d, block, block).wait_recv()

            loop(self.count, body)
            self.received = True

        def total(self, own_part):
            if not self.received:
                self.recv()
            total = own_part.astype(F32)
            for d in range(1, self.count):
                total = total + self.dst[lax.rem(self.me + self.count - d, self.count)].astype(F32)
            return total

        def finish(self):
            if not self.received:
                self.recv()
            loop(self.count, lambda d: self.copy(d, self.dst.at[0], self.dst.at[0]).wait_send())

    class Plane:
        def __init__(self, buf, first, second, sems, whole):
            self.buf, self.whole = buf, whole
            (self.me1, self.n1, self.peer1), (self.me2, self.n2, self.peer2) = first, second
            self.s1, self.r1, self.s2, self.r2 = sems
            self.forwarded, self.got = False, set()
            comms.append(self)

        def place(self, i, j):
            return j * self.n1 + i

        def line(self, d, j):
            group = self.buf.at[pl.ds(j * self.n1, self.n1)]
            return remote(group, group, self.s2.at[d, 0], self.r2.at[d, 0], self.peer2(d))

        def hop1(self, d, block):
            return remote(block, block, self.s1.at[d], self.r1.at[d], self.peer1(d))

        def hop2(self, d, i, block):
            return remote(block, block, self.s2.at[d, i], self.r2.at[d, i], self.peer2(d))

        def onward(self, i):
            block = self.buf.at[self.place(i, self.me2)]
            loop(self.n2, lambda d: self.hop2(d, i, block).start())

        def start(self):
            block = self.buf.at[self.place(self.me1, self.me2)]
            if not self.whole:
                self.onward(self.me1)
            loop(self.n1, lambda d: self.hop1(d, block).start())
            return self

        def forward(self):
            def body(d):
                i = lax.rem(self.me1 + self.n1 - d, self.n1)
                self.hop1(d, self.buf.at[self.place(i, self.me2)]).wait_recv()
                if not self.whole:
                    self.onward(i)

            loop(self.n1, body)
            if self.whole:
                loop(self.n2, lambda d: self.line(d, self.me2).start())
            self.forwarded = True

        def each(self, body):
            def step(i, carry):
                body(i)
                return carry

            lax.fori_loop(0, self.n1, step, 0)

        def arrived(self, d):
            source = lax.rem(self.me2 + self.n2 - d, self.n2)
            if self.whole:
                self.line(d, source).wait_recv()
            else:
                self.each(
                    lambda i: self.hop2(d, i, self.buf.at[self.place(i, source)]).wait_recv())
            self.got.add(d)

        def recv(self):
            if not self.forwarded:
                self.forward()
            for d in range(1, self.n2):
                if d not in self.got:
                    self.arrived(d)

        def finish(self):
            self.recv()
            block = self.buf.at[0]
            loop(self.n1, lambda d: self.hop1(d, block).wait_send())
            if self.whole:
                loop(self.n2, lambda d: self.line(d, 0).wait_send())
            else:
                self.each(lambda i: loop(self.n2, lambda d: self.hop2(d, i, block).wait_send()))

    def over_tp(buf, sems, whole):
        return Plane(buf, (z, Z, z_peer), (x, X, x_peer), sems, whole)

    def over_streams(buf, sems):
        return Plane(buf, (y, Y, y_peer), (core, 2, core_peer), sems, True)

    small[0].wait()
    own_up.wait()
    gain_row = jnp.concatenate([gain[0:1, :], gain[1:2, :]], axis=1)
    UT[me_t] = (first[...].astype(F32) * gain_row).astype(BF16)
    pl.semaphore_wait(barrier, Y + Z + X - 2)
    ups = over_tp(UT, ut_sems, False).start()
    for copy in (locals_[0], locals_[3], locals_[4], locals_[6], locals_[5]):
        copy.start()

    locals_[2].wait()
    kv_heads = wkv.shape[1] // (2 * HD)
    partial = dot(UT[me_t], wkv[...]).astype(BF16)
    for j in range(kv_heads):
        KP[j] = jnp.concatenate(
            [partial[:, j * HD:(j + 1) * HD], partial[:, (kv_heads + j) * HD:(kv_heads + j + 1) * HD]],
            axis=1,
        )
    kv_x = Axis(KP, KX, x, X, x_peer, kx_s, kx_r).start()

    for copy in small[1:]:
        copy.wait()
    steps = hidden.shape[1]
    lanes = iota((16, HD), 1)
    marks = jnp.zeros((16, HD), F32)
    last = jnp.int32(-1)
    step_of_row = iota((16, 1), 0) % 4
    last_col = jnp.full((16, 1), -1, I32)
    for u in range(steps):
        mark = flags[0, u]
        marks = marks + jnp.where(lanes % 4 == u, mark.astype(F32), 0.0)
        last = jnp.where(mark > 0, jnp.int32(u), last)
        last_col = jnp.where(step_of_row == u, last, last_col)

    locals_[1].wait()
    kn[...] = jnp.zeros_like(kn)
    for i in range(2):
        for hh in range(4):
            qs[pl.ds(i * 16 + hh * 4, 4), :] = qkv[0, :, pl.ds((i * 4 + hh) * HD, HD)].astype(F32)
        kn[i, 0:4, :] = qkv[0, :, pl.ds((8 + i) * HD, HD)].astype(F32)
        kn[2 + i, 0:4, :] = qkv[0, :, pl.ds((10 + i) * HD, HD)].astype(F32)
    length = bc.shape[0]
    scaling = HD ** (-0.5)
    seen = iota((16, length), 1) < byte_len[0, 0]
    causal = iota((16, 16), 1) <= iota((16, 16), 0) % 4
    for i in range(2):
        q_i = qs[pl.ds(i * 16, 16), :].astype(BF16)
        old = dot_t(q_i, bc[:, pl.ds(i * HD, HD)]) * scaling
        old = jnp.where(seen, old, NEG_FILL)
        new = dot_t(q_i, kn[i].astype(BF16)) * scaling
        new = jnp.where(causal, new, NEG_FILL)
        top = jnp.maximum(jnp.max(old, axis=1, keepdims=True), jnp.max(new, axis=1, keepdims=True))
        old, new = jnp.exp(old - top), jnp.exp(new - top)
        total = jnp.sum(old, axis=1, keepdims=True) + jnp.sum(new, axis=1, keepdims=True)
        old, new = (old / total).astype(BF16), (new / total).astype(BF16)
        os[pl.ds(i * 16, 16), :] = dot(old, bc[:, pl.ds((2 + i) * HD, HD)]) + dot(
            new, kn[2 + i].astype(BF16))
        for hh in range(4):
            xm[pl.ds((2 * i + hh // 2) * 4, 4), pl.ds((hh % 2) * HD, HD)] = (
                hidden[0, :, pl.ds((i * 4 + hh) * HD, HD)].astype(F32) + os[pl.ds(i * 16 + hh * 4, 4), :]
            )
    rows_16 = xm[...].astype(BF16)
    XS[me_p] = jnp.concatenate([rows_16, marks.astype(BF16)], axis=1)
    rows_s = over_streams(XS, xs_sems).start()

    ups.forward()
    rows_s.forward()

    tiles = kv_x.total(KP[x]).astype(BF16)
    tall = rows_own // 16
    for b in range(2 * tall):
        KS[b // (2 * tall // Z), b % (2 * tall // Z)] = tiles[
            (b // 2) * 16:(b // 2 + 1) * 16, (b % 2) * HD:(b % 2 + 1) * HD]
    kv_z = Axis(KS, KZ, z, Z, z_peer, kz_s, kz_r).start()

    o_col = jnp.sum(
        jnp.where(iota((S, T), 1) == me_t, owners[...].astype(F32), 0.0), axis=1, keepdims=True)
    eye = iota((S, S), 0) == iota((S, S), 1)
    o_row = jnp.sum(jnp.where(eye, o_col, 0.0), axis=0, keepdims=True)
    same = o_col == o_row
    rank_col = jnp.sum(
        jnp.where(same & (iota((S, S), 1) < iota((S, S), 0)), 1.0, 0.0), axis=1, keepdims=True)
    own_col = iota((S, 1), 0) == me_s
    my_owner = jnp.sum(jnp.where(own_col, o_col, 0.0), axis=0, keepdims=True)
    my_rank = jnp.sum(jnp.where(own_col, rank_col, 0.0), axis=0, keepdims=True)
    tgt_col = jnp.where(o_col == me_s.astype(F32), rank_col, -1.0)
    W = S * 16
    stream_of = lambda lane: (lane // 16 % Y) * 2 + lane // (16 * Y)
    tgt = jnp.sum(
        jnp.where(stream_of(iota((S, W), 1)) == iota((S, W), 0), tgt_col, 0.0), axis=0, keepdims=True)

    rows_s.recv()
    r, l = iota((16, W), 0), iota((16, W), 1)
    every = XS[...].reshape(W, 256 + HD)
    picked = (tgt == ((r % 8) // 4).astype(F32)) & (l % 4 == r % 4)
    halves = []
    for part in range(2):
        pick = jnp.where(picked & ((l % 16) // 4 == (r // 8) * 2 + part), 1.0, 0.0).astype(BF16)
        halves.append(dot(pick, every[:, :256]).astype(BF16))
    XT[me_t] = jnp.concatenate(halves, axis=1)
    rows_t = over_tp(XT, xt_sems, True).start()
    slot_marks = []
    for j in range(2):
        pick = jnp.where((tgt == float(j)) & (l % 16 == 0), 1.0, 0.0).astype(BF16)
        slot_marks.append(dot(pick, every[:, 256:]))
    slot_marks = jnp.where((lanes % 8) // 4 == 0, slot_marks[0], slot_marks[1])[0:8, :]

    locals_[3].wait()

    def query_part(source, total):
        base = pl.multiple_of(source * (Z * 256), Z * 256)
        for zb in range(Z):
            total = total + dot(UT[source * Z + zb], wq[pl.ds(base + zb * 256, 256), :])
        return total

    folded = query_part(x, jnp.zeros((rows_own, HD), F32))
    KA[z] = kv_z.total(KS[z]).astype(BF16)
    kv_all = Axis(KA, KA, z, Z, z_peer, ka_s, ka_r).start()
    rows_t.forward()
    for d in range(1, X):
        ups.arrived(d)
        folded = query_part(lax.rem(x + X - d, X), folded)
        if d == 1:
            kv_all.recv()
            for b in range(2 * tall):
                MK[me_p, pl.ds((b // 2) * 16, 16), pl.ds((b % 2) * HD, HD)] = KA[
                    b // (2 * tall // Z), b % (2 * tall // Z)]
            keyvals_s = over_streams(MK, mk_sems).start()
    MQ[me_p] = folded.astype(BF16)
    queries_s = over_streams(MQ, mq_sems).start()

    locals_[0].wait()
    rows_t.recv()
    rows_all = XT[...].reshape(T * 16, 512)
    N = T * 8

    def project(top, bottom, width):
        upper = dot(rows_all, top).reshape(T, 16, width)[:, :8]
        lower = dot(rows_all, bottom).reshape(T, 16, width)[:, 8:]
        return (upper + lower).reshape(N, width)

    expanded = project(up[0:512, :], up[512:1024, :], up.shape[1]).astype(BF16).astype(F32)
    squared = expanded * expanded
    high = squared.astype(BF16)
    low = (squared - high.astype(F32)).astype(BF16)
    ones = jnp.ones((8, up.shape[1]), BF16)
    spot = slot_marks[:, :N] if N <= HD else jnp.concatenate([slot_marks] * (N // HD), axis=1)
    spot = jnp.where(iota((8, N), 1) // 8 == me_t, spot, 0.0)
    SQZ[z] = jnp.where(iota((8, N), 0) == 0, dot_t(ones, high) + dot_t(ones, low), spot)
    squares_z = Axis(SQZ, SQZ, z, Z, z_peer, sqz_s, sqz_r).start()
    keyvals_s.forward()
    queries_s.forward()
    SQX[x] = squares_z.total(SQZ[z])
    squares_x = Axis(SQX, SQX, x, X, x_peer, sqx_s, sqx_r).start()

    keyvals_s.recv()
    weights = MK[...].reshape(S * rows_own, 2 * HD)
    keyvals = project(weights[:512], weights[512:], 2 * HD)
    keys = keyvals[:, :HD].astype(BF16)
    queries_s.recv()
    weights = MQ[...].reshape(S * rows_own, HD)
    raw[...] = project(weights[:512], weights[512:], HD)

    locals_[4].wait()
    locals_[6].wait()
    locals_[5].wait()
    slots, span = ck.shape[0], ck.shape[1]
    len_col = jnp.sum(
        jnp.where(iota((N, slots), 0) // 4 == iota((N, slots), 1), coarse_len[...].astype(F32), 0.0),
        axis=1, keepdims=True)
    summed = squares_x.total(SQX[x])
    inverse_row = lax.rsqrt(summed[0:1, :] / (up.shape[1] * T) + EPSILON)
    marked = summed[1:2, :] > 0.5
    inverse = jnp.sum(
        jnp.where(iota((N, N), 0) == iota((N, N), 1), inverse_row, 0.0), axis=1, keepdims=True)
    cols[...] = jnp.where(iota((N, HD), 1) == 0, inverse, len_col)
    values = (keyvals[:, HD:] * inverse).astype(BF16)

    block, per = Z * 8, min(8, Z * 2)
    chunks = Z * 2 // per
    by_chunk = lambda col: col.reshape(chunks, per * 4, 1)
    row_old, lane_old = iota((per * 4, per * span), 0), iota((per * 4, per * span), 1)
    position = jnp.where(lane_old // span == row_old // 4, lane_old % span, span).astype(F32)
    lane_new, row_new = iota((block, N), 1), iota((block, N), 0)
    back_x = Axis(PX, RX, x, X, x_peer, px_s, px_r)
    for d in list(range(1, X)) + [0]:
        to = lax.rem(x + d, X)
        at_row = pl.ds(pl.multiple_of(to * block, block), block)
        at_slot = pl.ds(to * (Z * 2), Z * 2)
        queries = raw[at_row, :].astype(BF16)
        factor, filled = cols[at_row, 0:1] * scaling, cols[at_row, 1:2]
        old = bdot_t(queries.reshape(chunks, per * 4, HD), ck[at_slot].reshape(chunks, per * span, HD))
        new = dot_t(queries, keys)
        row = row_new + to * block
        allowed = (lane_new // 4 == row // 4) & (lane_new % 4 <= row % 4) & marked
        old = jnp.where(position[None] < by_chunk(filled), old * by_chunk(factor), NEG_FILL)
        new = jnp.where(allowed, new * factor * inverse_row, NEG_FILL)
        top = jnp.maximum(
            jnp.max(old, axis=2, keepdims=True).reshape(block, 1), jnp.max(new, axis=1, keepdims=True))
        old, new = jnp.exp(old - by_chunk(top)), jnp.exp(new - top)
        total = jnp.sum(old, axis=2, keepdims=True).reshape(block, 1) + jnp.sum(
            new, axis=1, keepdims=True)
        old, new = (old / by_chunk(total)).astype(BF16), (new / total).astype(BF16)
        attended = bdot(old, cv[at_slot].reshape(chunks, per * span, HD)).reshape(block, HD)
        attended = (attended + dot(new, values)).astype(BF16)
        PX[to] = dot(attended, wr[...]).astype(BF16)
        if d:
            back_x.copy(d, PX.at[to], RX.at[x]).start()

    summed = back_x.total(PX[x]).reshape(Z, 8, 1024)
    PZ[...] = jnp.concatenate([summed[:, :, :512], summed[:, :, 512:]], axis=1).astype(BF16)
    back_z = Axis(PZ, RZ, z, Z, z_peer, pz_s, pz_r).start()
    RB[me_p] = back_z.total(PZ[z]).astype(BF16)
    back_s = over_streams(RB, rb_sems).start()
    back_s.recv()

    home = (stream_of(l).astype(F32) == my_owner) & (((l % 8) // 4).astype(F32) == my_rank)
    home = home & (l % 4 == last_col) & ((l % 16) // 8 == r // 8)
    back = RB[...].reshape(W, 512)
    latest = jnp.zeros((16, 256), F32)
    for part in range(2):
        pick = jnp.where(home & ((r // 4) % 2 == part), 1.0, 0.0).astype(BF16)
        latest = latest + dot(pick, back[:, part * 256:(part + 1) * 256])
    earlier = jnp.zeros((16, 256), F32)
    for k in range(4):
        earlier = jnp.where(
            iota((16, 256), 0) // 4 == k, prev[0:1, pl.ds(k * 256, 256)].astype(F32), earlier)
    latest = jnp.where(last_col < 0, earlier, latest)
    xm[...] = rows_16.astype(F32) + latest
    for k in range(4):
        out_ref[0, :, pl.ds(k * 256, 256)] = xm[pl.ds(k * 4, 4), :].astype(BF16)

    for comm in comms:
        comm.finish()


def shards(
    S, X, Z,
    hidden_in, byte_qkv, byte_cache, byte_len, flags, coarse_prev, owner_map, up_weight,
    coarse_gain, query_weight, keyval_weight, return_weight, coarse_cache, coarse_len,
):
    T = X * Z
    part = up_weight.shape[1]
    gains = coarse_gain.reshape(T, part // HD, HD)
    owners = owner_map.transpose(1, 2, 0)
    rows = up_weight.shape[0] // S
    heads2 = 2 * HD
    vm = pl.BlockSpec(memory_space=pltpu.VMEM)
    hbm = pl.BlockSpec(memory_space=pl.ANY)
    dma = pltpu.SemaphoreType.DMA
    pair = lambda *shape: [dma(shape), dma(shape)]
    scratch = [
        pltpu.SMEM((1, 1), I32),
        pltpu.SMEM(flags.shape, I32),
        pltpu.VMEM(hidden_in.shape, BF16),
        pltpu.VMEM(byte_qkv.shape, BF16),
        pltpu.VMEM(coarse_prev.shape, BF16),
        pltpu.VMEM((S, T), I32),
        pltpu.VMEM(gains.shape[1:], F32),
        pltpu.VMEM(coarse_len.shape, I32),
        pltpu.VMEM((rows, part), BF16),
        pltpu.VMEM(byte_cache.shape[1:], BF16),
        pltpu.VMEM(up_weight.shape, BF16),
        pltpu.VMEM(query_weight.shape, BF16),
        pltpu.VMEM(keyval_weight.shape, BF16),
        pltpu.VMEM(return_weight.shape, BF16),
        pltpu.VMEM((coarse_cache.shape[1], coarse_cache.shape[3], HD), BF16),
        pltpu.VMEM((coarse_cache.shape[1], coarse_cache.shape[3], HD), BF16),
        pltpu.VMEM((32, HD), F32),
        pltpu.VMEM((4, 16, HD), F32),
        pltpu.VMEM((32, HD), F32),
        pltpu.VMEM((16, 256), F32),
        pltpu.VMEM((T * 8, HD), F32),
        pltpu.VMEM((T * 8, HD), F32),
        pltpu.VMEM((S, 16, 256 + HD), BF16),
        pltpu.VMEM((T, 16, 512), BF16),
        pltpu.VMEM((T, rows, part), BF16),
        pltpu.VMEM((S, rows, HD), BF16),
        pltpu.VMEM((S, rows, heads2), BF16),
        pltpu.VMEM((X, rows, heads2), BF16),
        pltpu.VMEM((X, rows, heads2), BF16),
        pltpu.VMEM((Z, rows // (8 * Z), 16, HD), BF16),
        pltpu.VMEM((Z, rows // (8 * Z), 16, HD), BF16),
        pltpu.VMEM((Z, rows // (8 * Z), 16, HD), BF16),
        pltpu.VMEM((Z, 8, T * 8), F32),
        pltpu.VMEM((X, 8, T * 8), F32),
        pltpu.VMEM((X, Z * 8, 1024), BF16),
        pltpu.VMEM((X, Z * 8, 1024), BF16),
        pltpu.VMEM((Z, 16, 512), BF16),
        pltpu.VMEM((Z, 16, 512), BF16),
        pltpu.VMEM((S, 16, 512), BF16),
        dma((16,)),
    ]
    Y = S // 2
    on_streams = [dma((Y,)), dma((Y,)), dma((2, 1)), dma((2, 1))]
    on_tp = [dma((Z,)), dma((Z,)), dma((X, Z)), dma((X, Z))]
    scratch += [on_streams, on_tp, on_tp] + [on_streams] * 3
    for shape in ((X,), (Z,), (Z,), (Z,), (X,), (X,), (Z,)):
        scratch += pair(*shape)
    return pl.pallas_call(
        functools.partial(kernel, S, X, Z),
        out_shape=jax.ShapeDtypeStruct(hidden_in.shape, BF16),
        in_specs=[hbm] * 14,
        out_specs=vm,
        scratch_shapes=scratch,
        compiler_params=pltpu.CompilerParams(
            collective_id=0, has_side_effects=True, vmem_limit_bytes=60 * 1024 * 1024
        ),
        name="decode",
    )(
        byte_len.reshape(1, 1), flags, hidden_in, byte_qkv, coarse_prev, owners, gains, coarse_len,
        byte_cache, up_weight, query_weight, keyval_weight, return_weight, coarse_cache,
    )


def solution(mesh):
    S, T = mesh.shape["streams"], mesh.shape["tp"]
    X = 4 if T >= 16 else 2
    return jax.shard_map(
        functools.partial(shards, S, X, T // X),
        mesh=mesh,
        in_specs=(
            P(("streams", "tp"), None, None),
            P(("streams", "tp"), None, None),
            P(("streams", "tp"), None, None),
            P(("streams", "tp")),
            P(("streams", "tp"), None),
            P(("streams", "tp"), None),
            P(),
            P(None, "tp"),
            P(),
            P(None, "tp"),
            P("tp", None),
            P("tp", None),
            P("streams", None, "tp", None, None),
            P("streams", None),
        ),
        out_specs=P(("streams", "tp"), None, None),
        check_vma=False,
    )
```

time: 98.1 us -> 75.9 us (0.77)
  Pallas kernels: 84.3 us -> 73.8 us
  local copies, waits for them, and re-layouts: 11.6 us -> 1.3 us
    pallas_call x1, Pallas kernels: 84.3 us -> 73.8 us  [shards(): pl.pallas_call(functools.partial(kernel, S, X, Z), out_shape=jax.ShapeDty...]
    unnamed x23 -> x1, local copies, waits for them, and re-layouts: 10.8 us -> 1.3 us
where the time goes in v2:
time: 75.9 us; the launch traced here: 75.8 us
  Pallas kernels  73.8 us (97%)
  local copies, waits for them, and re-layouts  1.3 us (2%)
    pallas_call x1, Pallas kernels, shards(): pl.pallas_call(functools.partial(kernel, S, X, Z), out_shape=jax.ShapeDty...  73.8 us

profile of v2, /device:TPU:1, one launch (start us, length us, event | category | flops | bytes accessed | tf_op | source)
XLA Modules:
  0.0 75.8 jit_solution(9439800582325563209)
XLA Ops:
  0.7 73.8 %decode.1 = bf16[1,4,1024]{2,1,0:T(4,128)(2,1)} custom-call(s32[1,1]{1,0:T(1,128)} %bitcast.3.byte_len_hbm, s32[1,4]{1,0:T(1,128)} %flags_hbm.1, bf16[1,4,1024]{2,1,0:T(4,128)(2,1)} %hidden_hbm.1, bf16[1,4,1536]{2,1,0:T(4,128)(2,1)} %qkv_hbm.1, bf16[1,1024]{1,0:T(2,128)(2,1)} %prev_hbm.1, s32[16,1,32]{2,1,0:T(1,128)} %bitcast.5, f32[32,2,128]{2,1,0:T(2,128)} %bitcast.4, ...), custom_call_target="tpu_custom_call" | custom-call | tf_op jit(solution)/shard_map/decode/pallas_call | solution.py:535
  74.5 1.3 %copy.17 = bf16[1,4,1024]{2,1,0:T(4,128)(2,1)} copy(bf16[1,4,1024]{2,1,0:T(4,128)(2,1)} %decode.1) | data formatting | bytes 16384

commit v3 on v2

--- a/solution.py
+++ b/solution.py
@@ -111,6 +111,9 @@
         loop(count, lambda d, peer=peer: pl.semaphore_signal(
             barrier, inc=1, device_id=peer(d), device_id_type=MESH))
 
+    def far_first(count):
+        return sorted(range(1, count), key=lambda d: -min(d, count - d))
+
     comms = []
 
     class Axis:
@@ -175,7 +178,8 @@
 
         def onward(self, i):
             block = self.buf.at[self.place(i, self.me2)]
-            loop(self.n2, lambda d: self.hop2(d, i, block).start())
+            for d in far_first(self.n2):
+                self.hop2(d, i, block).start()
 
         def start(self):
             block = self.buf.at[self.place(self.me1, self.me2)]
@@ -418,7 +422,7 @@
     position = jnp.where(lane_old // span == row_old // 4, lane_old % span, span).astype(F32)
     lane_new, row_new = iota((block, N), 1), iota((block, N), 0)
     back_x = Axis(PX, RX, x, X, x_peer, px_s, px_r)
-    for d in list(range(1, X)) + [0]:
+    for d in far_first(X) + [0]:
         to = lax.rem(x + d, X)
         at_row = pl.ds(pl.multiple_of(to * block, block), block)
         at_slot = pl.ds(to * (Z * 2), Z * 2)
@@ -442,6 +446,10 @@
         if d:
             back_x.copy(d, PX.at[to], RX.at[x]).start()
 
+    for comm in comms:
+        if comm is not back_x:
+            comm.finish()
+
     summed = back_x.total(PX[x]).reshape(Z, 8, 1024)
     PZ[...] = jnp.concatenate([summed[:, :, :512], summed[:, :, 512:]], axis=1).astype(BF16)
     back_z = Axis(PZ, RZ, z, Z, z_peer, pz_s, pz_r).start()
@@ -465,7 +473,7 @@
     for k in range(4):
         out_ref[0, :, pl.ds(k * 256, 256)] = xm[pl.ds(k * 4, 4), :].astype(BF16)
 
-    for comm in comms:
+    for comm in (back_x, back_z, back_s):
         comm.finish()
 
 
@@ -481,7 +489,6 @@
     rows = up_weight.shape[0] // S
     heads2 = 2 * HD
     vm = pl.BlockSpec(memory_space=pltpu.VMEM)
-    hbm = pl.BlockSpec(memory_space=pl.ANY)
     dma = pltpu.SemaphoreType.DMA
     pair = lambda *shape: [dma(shape), dma(shape)]
     scratch = [
@@ -535,7 +542,7 @@
     return pl.pallas_call(
         functools.partial(kernel, S, X, Z),
         out_shape=jax.ShapeDtypeStruct(hidden_in.shape, BF16),
-        in_specs=[hbm] * 14,
+        in_specs=[pl.BlockSpec(memory_space=pltpu.HBM)] * 14,
         out_specs=vm,
         scratch_shapes=scratch,
         compiler_params=pltpu.CompilerParams(

time: 75.9 us -> 75.3 us (level)
  no operation moved by 1% of the time
where the time goes in v3:
time: 75.3 us; the launch traced here: 75.1 us
  Pallas kernels  73.1 us (97%)
  local copies, waits for them, and re-layouts  1.3 us (2%)
    pallas_call x1, Pallas kernels, shards(): pl.pallas_call(functools.partial(kernel, S, X, Z), out_shape=jax.ShapeDty...  73.1 us

profile of v3, /device:TPU:1, one launch (start us, length us, event | category | flops | bytes accessed | tf_op | source)
XLA Modules:
  0.0 75.1 jit_solution(13499522242540431344)
XLA Ops:
  0.7 73.1 %decode.1 = bf16[1,4,1024]{2,1,0:T(4,128)(2,1)} custom-call(s32[1,1]{1,0:T(1,128)} %bitcast.3.byte_len_hbm, s32[1,4]{1,0:T(1,128)} %flags_hbm.1, bf16[1,4,1024]{2,1,0:T(4,128)(2,1)} %hidden_hbm.1, bf16[1,4,1536]{2,1,0:T(4,128)(2,1)} %qkv_hbm.1, bf16[1,1024]{1,0:T(2,128)(2,1)} %prev_hbm.1, s32[16,1,32]{2,1,0:T(1,128)} %bitcast.5, f32[32,2,128]{2,1,0:T(2,128)} %bitcast.4, ...), custom_call_target="tpu_custom_call" | custom-call | tf_op jit(solution)/shard_map/decode/pallas_call | solution.py:542
  73.8 1.3 %copy.17 = bf16[1,4,1024]{2,1,0:T(4,128)(2,1)} copy(bf16[1,4,1024]{2,1,0:T(4,128)(2,1)} %decode.1) | data formatting | bytes 16384

commit v4 on v3

--- a/solution.py
+++ b/solution.py
@@ -94,11 +94,8 @@
         return (me_s, lax.rem(x + d, X) * Z + z)
 
     def loop(count, body):
-        def step(d, carry):
+        for d in range(1, count):
             body(d)
-            return carry
-
-        lax.fori_loop(1, count, step, 0)
 
     def remote(src, dst, send, recv, peer):
         return pltpu.make_async_remote_copy(

time: 75.3 us -> 75.1 us (level)
  no operation moved by 1% of the time
where the time goes in v4:
time: 75.1 us; the launch traced here: 74.9 us
  Pallas kernels  72.9 us (97%)
  local copies, waits for them, and re-layouts  1.3 us (2%)
    pallas_call x1, Pallas kernels, shards(): pl.pallas_call(functools.partial(kernel, S, X, Z), out_shape=jax.ShapeDty...  72.9 us

profile of v4, /device:TPU:1, one launch (start us, length us, event | category | flops | bytes accessed | tf_op | source)
XLA Modules:
  0.0 74.9 jit_solution(17353285842892672378)
XLA Ops:
  0.7 72.9 %decode.1 = bf16[1,4,1024]{2,1,0:T(4,128)(2,1)} custom-call(s32[1,1]{1,0:T(1,128)} %bitcast.3.byte_len_hbm, s32[1,4]{1,0:T(1,128)} %flags_hbm.1, bf16[1,4,1024]{2,1,0:T(4,128)(2,1)} %hidden_hbm.1, bf16[1,4,1536]{2,1,0:T(4,128)(2,1)} %qkv_hbm.1, bf16[1,1024]{1,0:T(2,128)(2,1)} %prev_hbm.1, s32[16,1,32]{2,1,0:T(1,128)} %bitcast.5, f32[32,2,128]{2,1,0:T(2,128)} %bitcast.4, ...), custom_call_target="tpu_custom_call" | custom-call | tf_op jit(solution)/shard_map/decode/pallas_call | solution.py:539
  73.6 1.3 %copy.17 = bf16[1,4,1024]{2,1,0:T(4,128)(2,1)} copy(bf16[1,4,1024]{2,1,0:T(4,128)(2,1)} %decode.1) | data formatting | bytes 16384
